TPU v7x, 512 devices: a whole 4x4x16 slice. The times are simulated.
512 devices in a mesh: row: 32 (over z, core), col: 16 (over x, y).
Axes of the slice: x: 4, y: 4, z: 16, core: 2. Of those that a mesh axis runs over, the one named last changes fastest.
Arguments:
- blocks: bfloat16 [16384, 128, 128], P(('row', 'col')), may hold values from -0.09375 to 0.09375
- block_rows: int32 [16384], P(('row', 'col')), may hold values from 0 to 512, as said below
- block_cols: int32 [16384], P(('row', 'col')), may hold values from 0 to 512, as said below
- start: float32 [64, 65536], P(None, ('row', 'col'))
Outputs:
- basis: float32 [64, 65536], P(None, ('row', 'col'))
- alphas: float32 [3, 64, 64], replicated
- betas: float32 [3, 64, 64], replicated
Inputs may be any that keep to these rules, and one draw needn't show every extreme that they name: For device d the entries d * 32 to (d + 1) * 32 - 1 list its stored blocks first and then empty slots, which hold 512 in both lists. A stored block (i, j) has i <= j, i // 16 equal to the device's row index, j % 16 equal to its col index, and no position is stored twice. The devices of row index 0 fill all 32 slots; block_cols holds 512 exactly where block_rows does. `block_cols`: see block_rows.
All inputs are finite; a program needn't handle non-finite values.
Results may differ from a plain program's by a relative error of at most 0.04.
Values may be sent and summed in bfloat16 or wider, within the bound.
A program may use at most 64 MiB of HBM per device.

v0:
```python
import jax
import jax.numpy as jnp
from jax import lax
from jax.sharding import PartitionSpec as P

ITERS = 3


HIGH = lax.Precision.HIGHEST


def local_inner(left, right):
    return jnp.dot(left, right.T, precision=HIGH)


def factorize(gramian, identity):
    factor_low = jnp.linalg.cholesky(gramian)
    inverse = jax.scipy.linalg.solve_triangular(factor_low, identity, lower=True)
    return (inverse, factor_low)


def shards(blocks, block_rows, block_cols, start):
    row_count = lax.axis_size("row")
    col_count = lax.axis_size("col")
    row_index = lax.axis_index("row")
    vec_width = start.shape[0]
    block_size = start.shape[1]
    columns_all = row_count * col_count * block_size
    identity = jnp.eye(vec_width, dtype=jnp.float32)
    row_target = block_rows - row_index * col_count
    col_target = block_cols // col_count
    hot_rows = row_target[:, None] == jnp.arange(col_count)[None, :]
    hot_cols = col_target[:, None] == jnp.arange(row_count)[None, :]
    gramian = lax.psum(local_inner(start, start), ("row", "col")) / columns_all
    inverse, factor_low = factorize(gramian, identity)
    basis = jnp.dot(inverse, start, precision=HIGH)
    previous = None
    alpha_list = []
    beta_list = []
    for step in range(ITERS):
        rounded = basis.astype(jnp.bfloat16)
        row_stripe = lax.all_gather(rounded, "col", axis=1, tiled=True).reshape(
            vec_width, col_count, block_size
        )
        column_set = lax.all_gather(rounded, "row", axis=1, tiled=True).reshape(
            vec_width, row_count, block_size
        )
        taken_cols = jnp.einsum(
            "kmb,sm->ksb",
            column_set,
            hot_cols.astype(jnp.bfloat16),
            preferred_element_type=jnp.float32,
        ).astype(jnp.bfloat16)
        taken_rows = jnp.einsum(
            "kmb,sm->ksb",
            row_stripe,
            hot_rows.astype(jnp.bfloat16),
            preferred_element_type=jnp.float32,
        ).astype(jnp.bfloat16)
        forward = jnp.einsum("ksb,sdb->ksd", taken_cols, blocks, preferred_element_type=jnp.float32)
        row_part = jnp.einsum("ksd,sm->kmd", forward, hot_rows.astype(jnp.float32), precision=HIGH)
        backward = jnp.einsum(
            "ksb,sbd->ksd", taken_rows, blocks, preferred_element_type=jnp.float32
        )
        col_part = jnp.einsum("ksd,sm->kmd", backward, hot_cols.astype(jnp.float32), precision=HIGH)
        own_rows = lax.psum_scatter(
            row_part.astype(jnp.bfloat16), "col", scatter_dimension=1, tiled=True
        ).astype(jnp.float32)
        own_cols = lax.psum_scatter(
            col_part.astype(jnp.bfloat16), "row", scatter_dimension=1, tiled=True
        ).astype(jnp.float32)
        residue = own_rows.reshape(vec_width, block_size) + own_cols.reshape(vec_width, block_size)
        if previous is not None:
            residue = residue - jnp.dot(factor_low.T, previous, precision=HIGH)
        alpha = lax.psum(local_inner(basis, residue), ("row", "col")) / columns_all
        residue = residue - jnp.dot(alpha.T, basis, precision=HIGH)
        gramian = lax.psum(local_inner(residue, residue), ("row", "col")) / columns_all
        inverse, factor_low = factorize(gramian, identity)
        alpha_list.append(alpha)
        beta_list.append(factor_low)
        previous = basis
        basis = jnp.dot(inverse, residue, precision=HIGH)
    return (basis, jnp.stack(alpha_list), jnp.stack(beta_list))


def solution(mesh):
    in_specs = (
        P(("row", "col"), None, None),
        P(("row", "col")),
        P(("row", "col")),
        P(None, ("row", "col")),
    )
    out_specs = (P(None, ("row", "col")), P(), P())
    return jax.shard_map(shards, mesh=mesh, in_specs=in_specs, out_specs=out_specs, check_vma=False)
```

profile of v0, /device:TPU:1, one launch (start us, length us, event | category | flops | bytes accessed | tf_op | source)
XLA Modules:
  0.0 1513.7 jit_solution(926172588916791671)
XLA Ops:
  7.2 1.0 fusion.127
  8.3 111.2 %psum.49 = f32[64,64]{0,1:T(8,128)S(1)} all-reduce(f32[64,64]{0,1:T(8,128)S(1)} %fusion.127), channel_id=1, replica_groups=mesh['row'=32,'col'=16] {'row','col'}, use_global_device_ids=true, to_apply=%region_0.1 | all-reduce | flops 4096 | bytes 32768 | tf_op jit(solution)/shard_map/psum | solution.py:34
  119.5 5.8 cholesky.74
  125.4 0.6 compare_reduce_fusion.3
  126.0 0.7 fusion.44
  126.7 4.9 custom-call.8
  131.9 0.5 copy-done.1
  132.6 0.6 copy-done.4
  133.2 29.9 %all_gather.18 = bf16[64,4096]{1,0:T(8,128)(2,1)S(1)} all-gather(bf16[64,128]{1,0:T(8,128)(2,1)S(1)} %get-tuple-element.17), channel_id=1, replica_groups=mesh['row'=32,'col'=16] {'row'}, dimensions={1}, use_global_device_ids=true | all-gather | bytes 540672 | tf_op jit(solution)/shard_map/all_gather | solution.py:45
  163.2 0.6 copy-done.5
  164.2 0.8 fusion.19
  165.0 1.1 fusion.3
  166.1 0.8 copy.21
  167.0 16.5 %all_gather.19 = bf16[64,2048]{1,0:T(8,128)(2,1)S(1)} all-gather(bf16[64,128]{1,0:T(8,128)(2,1)S(1)} %get-tuple-element.17), channel_id=1, replica_groups=mesh['row'=32,'col'=16] {'col'}, dimensions={1}, use_global_device_ids=true | all-gather | bytes 278528 | tf_op jit(solution)/shard_map/all_gather | solution.py:42
  183.9 0.4 fusion.22
  184.3 1.3 fusion
  185.6 1.0 copy.22
  186.6 58.9 %reduce-scatter.19.cloned.1.call-done = bf16[64,1,128]{2,0,1:T(8,128)(2,1)} async-done(((bf16[64,16,128]{2,0,1:T(8,128)(2,1)}), bf16[64,1,128]{2,0,1:T(8,128)(2,1)}) %reduce-scatter.19.cloned.1.call-update) | async-done | bytes 16400
  245.6 108.3 %reduce-scatter.13.cloned.1.call-done = bf16[64,1,128]{2,0,1:T(8,128)(2,1)} async-done(((bf16[64,32,128]{2,0,1:T(8,128)(2,1)}), bf16[64,1,128]{2,0,1:T(8,128)(2,1)}) %reduce-scatter.13.cloned.1.call-update) | async-done | bytes 16400 | tf_op jit(solution)/shard_map/reduce_scatter | solution.py:69
  353.9 0.9 fusion.51
  354.8 106.5 %psum.50 = f32[64,64]{0,1:T(8,128)S(1)} all-reduce(f32[64,64]{0,1:T(8,128)S(1)} %fusion.51), channel_id=1, replica_groups=mesh['row'=32,'col'=16] {'row','col'}, use_global_device_ids=true, to_apply=%region_5.8 | all-reduce | flops 4096 | bytes 32768 | tf_op jit(solution)/shard_map/psum | solution.py:75
  461.7 98.9 %psum.51 = f32[64,64]{0,1:T(8,128)S(1)} all-reduce(f32[64,64]{0,1:T(8,128)S(1)} %fusion.128), channel_id=1, replica_groups=mesh['row'=32,'col'=16] {'row','col'}, use_global_device_ids=true, to_apply=%region_6.9 | all-reduce | flops 4096 | bytes 32768 | tf_op jit(solution)/shard_map/psum | solution.py:77
  560.7 5.8 cholesky.85
  566.6 0.6 compare_reduce_fusion.2
  567.2 0.7 fusion.74
  567.9 4.9 custom-call.9
  573.2 31.9 %all_gather.20 = bf16[64,4096]{1,0:T(8,128)(2,1)S(1)} all-gather(bf16[64,128]{1,0:T(8,128)(2,1)S(1)} %get-tuple-element.19), channel_id=1, replica_groups=mesh['row'=32,'col'=16] {'row'}, dimensions={1}, use_global_device_ids=true | all-gather | bytes 540672 | tf_op jit(solution)/shard_map/all_gather | solution.py:45
  605.0 17.4 %all_gather.21 = bf16[64,2048]{1,0:T(8,128)(2,1)S(1)} all-gather(bf16[64,128]{1,0:T(8,128)(2,1)S(1)} %get-tuple-element.19), channel_id=1, replica_groups=mesh['row'=32,'col'=16] {'col'}, dimensions={1}, use_global_device_ids=true | all-gather | bytes 278528 | tf_op jit(solution)/shard_map/all_gather | solution.py:42
  622.9 0.8 fusion.25
  623.8 1.1 fusion.4
  624.8 0.8 copy.26
  626.1 0.4 fusion.28
  626.5 1.3 fusion.1
  627.8 1.0 copy.27
  628.8 81.9 %reduce-scatter.21.cloned.1.call-done = bf16[64,1,128]{2,0,1:T(8,128)(2,1)} async-done(((bf16[64,16,128]{2,0,1:T(8,128)(2,1)}), bf16[64,1,128]{2,0,1:T(8,128)(2,1)}) %reduce-scatter.21.cloned.1.call-update) | async-done | bytes 16400
  710.7 108.1 %reduce-scatter.15.cloned.1.call-done = bf16[64,1,128]{2,0,1:T(8,128)(2,1)} async-done(((bf16[64,32,128]{2,0,1:T(8,128)(2,1)}), bf16[64,1,128]{2,0,1:T(8,128)(2,1)}) %reduce-scatter.15.cloned.1.call-update) | async-done | bytes 16400 | tf_op jit(solution)/shard_map/reduce_scatter | solution.py:69
  818.8 1.6 convolution_subtract_fusion.3
  820.7 106.2 %psum.52 = f32[64,64]{0,1:T(8,128)S(1)} all-reduce(f32[64,64]{0,1:T(8,128)S(1)} %fusion.129), channel_id=1, replica_groups=mesh['row'=32,'col'=16] {'row','col'}, use_global_device_ids=true, to_apply=%region_9.12 | all-reduce | flops 4096 | bytes 32768 | tf_op jit(solution)/shard_map/psum | solution.py:75
  927.2 98.9 %psum.53 = f32[64,64]{0,1:T(8,128)S(1)} all-reduce(f32[64,64]{0,1:T(8,128)S(1)} %fusion.130), channel_id=1, replica_groups=mesh['row'=32,'col'=16] {'row','col'}, use_global_device_ids=true, to_apply=%region_10.13 | all-reduce | flops 4096 | bytes 32768 | tf_op jit(solution)/shard_map/psum | solution.py:77
  1026.2 5.8 cholesky.96
  1032.1 0.6 compare_reduce_fusion.1
  1032.8 0.7 fusion.72
  1033.4 4.9 custom-call.10
  1038.7 31.9 %all_gather.22 = bf16[64,4096]{1,0:T(8,128)(2,1)S(1)} all-gather(bf16[64,128]{1,0:T(8,128)(2,1)S(1)} %get-tuple-element.21), channel_id=1, replica_groups=mesh['row'=32,'col'=16] {'row'}, dimensions={1}, use_global_device_ids=true | all-gather | bytes 540672 | tf_op jit(solution)/shard_map/all_gather | solution.py:45
  1070.6 17.6 %all_gather.23 = bf16[64,2048]{1,0:T(8,128)(2,1)S(1)} all-gather(bf16[64,128]{1,0:T(8,128)(2,1)S(1)} %get-tuple-element.21), channel_id=1, replica_groups=mesh['row'=32,'col'=16] {'col'}, dimensions={1}, use_global_device_ids=true | all-gather | bytes 278528 | tf_op jit(solution)/shard_map/all_gather | solution.py:42
  1088.3 0.4 fusion.85
  1088.7 0.8 fusion.31
  1089.5 1.1 fusion.5
  1090.6 0.8 copy.31
  1091.8 0.4 fusion.34
  1092.2 1.3 fusion.2
  1093.5 1.0 copy.32
  1094.5 81.9 %reduce-scatter.23.cloned.1.call-done = bf16[64,1,128]{2,0,1:T(8,128)(2,1)} async-done(((bf16[64,16,128]{2,0,1:T(8,128)(2,1)}), bf16[64,1,128]{2,0,1:T(8,128)(2,1)}) %reduce-scatter.23.cloned.1.call-update) | async-done | bytes 16400
  1176.4 108.4 %reduce-scatter.17.cloned.1.call-done = bf16[64,1,128]{2,0,1:T(8,128)(2,1)} async-done(((bf16[64,32,128]{2,0,1:T(8,128)(2,1)}), bf16[64,1,128]{2,0,1:T(8,128)(2,1)}) %reduce-scatter.17.cloned.1.call-update) | async-done | bytes 16400 | tf_op jit(solution)/shard_map/reduce_scatter | solution.py:69
  1284.9 1.6 convolution_subtract_fusion.1
  1286.7 106.3 %psum.54 = f32[64,64]{0,1:T(8,128)S(1)} all-reduce(f32[64,64]{0,1:T(8,128)S(1)} %fusion.131), channel_id=1, replica_groups=mesh['row'=32,'col'=16] {'row','col'}, use_global_device_ids=true, to_apply=%region_13.16 | all-reduce | flops 4096 | bytes 32768 | tf_op jit(solution)/shard_map/psum | solution.py:75
  1393.3 98.9 %psum.55 = f32[64,64]{0,1:T(8,128)S(1)} all-reduce(f32[64,64]{0,1:T(8,128)S(1)} %fusion.132), channel_id=1, replica_groups=mesh['row'=32,'col'=16] {'row','col'}, use_global_device_ids=true, to_apply=%region_14.17 | all-reduce | flops 4096 | bytes 32768 | tf_op jit(solution)/shard_map/psum | solution.py:77
  1492.3 5.8 cholesky.107
  1498.2 0.6 compare_reduce_fusion
  1498.9 0.7 fusion.71
  1499.5 0.7 copy.36
  1500.3 4.9 custom-call.11
  1505.4 0.8 fusion.133
  1506.2 0.6 pad_maximum_fusion.1
  (69 shorter events, 5.9 us)
Async XLA Ops:
  7.2 157.0 %copy-start = (bf16[32,128,128]{2,1,0:T(8,128)(2,1)S(1)}, bf16[32,128,128]{2,1,0:T(8,128)(2,1)}, u32[]{:S(2)}) copy-start(bf16[32,128,128]{2,1,0:T(8,128)(2,1)} %param.7) | copy-start | bytes 3145732
  7.2 238.4 %reduce-scatter.19.cloned.1.call-start = ((), (), s32[]{:S(2)}) async-start(), calls=%async_computation.9 | async-start | bytes 278528
  131.6 0.8 copy-start.1
  132.6 0.7 copy-start.4
  163.2 0.7 copy-start.5
  166.9 187.0 %reduce-scatter.13.cloned.1.call-start = ((), (), s32[]{:S(2)}) async-start(), calls=%async_computation.6 | async-start | bytes 540672 | tf_op jit(solution)/shard_map/reduce_scatter | solution.py:69
  186.6 524.1 %reduce-scatter.21.cloned.1.call-start = ((), (), s32[]{:S(2)}) async-start(), calls=%async_computation.10 | async-start | bytes 278528
  354.8 106.5 %copy-start.2 = (bf16[64,1,128]{2,0,1:T(8,128)(2,1)S(1)}, bf16[64,1,128]{2,0,1:T(8,128)(2,1)}, u32[]{:S(2)}) copy-start(bf16[64,1,128]{2,0,1:T(8,128)(2,1)} %reduce-scatter.19.cloned.1.call-done) | copy-start | bytes 49156
  354.8 106.5 %copy-start.3 = (bf16[64,1,128]{2,0,1:T(8,128)(2,1)S(1)}, bf16[64,1,128]{2,0,1:T(8,128)(2,1)}, u32[]{:S(2)}) copy-start(bf16[64,1,128]{2,0,1:T(8,128)(2,1)} %reduce-scatter.13.cloned.1.call-done) | copy-start | bytes 49156
  625.6 193.2 %reduce-scatter.15.cloned.1.call-start = ((), (), s32[]{:S(2)}) async-start(), calls=%async_computation.7 | async-start | bytes 540672 | tf_op jit(solution)/shard_map/reduce_scatter | solution.py:69
  628.8 547.7 %reduce-scatter.23.cloned.1.call-start = ((), (), s32[]{:S(2)}) async-start(), calls=%async_computation.11 | async-start | bytes 278528
  1091.4 193.5 %reduce-scatter.17.cloned.1.call-start = ((), (), s32[]{:S(2)}) async-start(), calls=%async_computation.8 | async-start | bytes 540672 | tf_op jit(solution)/shard_map/reduce_scatter | solution.py:69
Sparse Core Ops, SparseCore 0:
  167.0 78.5 reduce-scatter.18
  248.6 105.2 reduce-scatter.12
  625.8 84.9 reduce-scatter.20
  713.6 105.2 reduce-scatter.14
  1091.5 84.9 reduce-scatter.22
  1179.3 105.5 reduce-scatter.16
where the time goes:
time: 1520 us; the launch traced here: 1510 us
  blocking collectives  872 us (57%)
  waiting for transfers between devices  548 us (36%)
  other arithmetic  49 us (3%)
  matrix products  21.6 us (1%)
    reduce_scatter x3, waiting for transfers between devices, shards(): lax.psum_scatter(col_part.astype(jnp.bfloat16), 'row', scatter_dimension=...  325 us
    psum x3, blocking collectives, shards(): alpha = lax.psum(local_inner(basis, residue), ('row', 'col')) / columns_all  319 us
    psum x3, blocking collectives, shards(): lax.psum(local_inner(residue, residue), ('row', 'col')) / columns_all  297 us
    unnamed x9, waiting for transfers between devices  223 us
    psum x1, blocking collectives, shards(): gramian = lax.psum(local_inner(start, start), ('row', 'col')) / columns_all  111 us
    all_gather x3, blocking collectives, shards(): lax.all_gather(rounded, 'row', axis=1, tiled=True)  93.6 us
    all_gather x3, blocking collectives, shards(): lax.all_gather(rounded, 'col', axis=1, tiled=True)  51.5 us
  transfers between devices with their start and end apart: 6, of which 6 were waited for; matrix products, arithmetic and copies ran while one was open for 1% of the time, Pallas kernels for 0%

commit v1 on v0

v1 whole, which is shorter than its diff:
```python
import jax
import jax.numpy as jnp
from jax import lax
from jax.experimental import pallas as pl
from jax.experimental.pallas import tpu as pltpu
from jax.sharding import PartitionSpec as P

ITERS = 3
HIGH = lax.Precision.HIGHEST
MESH = pl.DeviceIdType.MESH
F32 = jnp.float32
BF16 = jnp.bfloat16

NZ = 16
NC = 16
SLOTS = 32
FAR = (8, 7, 9, 6, 10, 5, 11, 4, 12, 3, 13, 2, 14, 1, 15)


def nt(a, b):
    return lax.dot_general(a, b, (((1,), (1,)), ((), ())), precision=HIGH, preferred_element_type=F32)


def nn(a, b):
    return lax.dot_general(a, b, (((1,), (0,)), ((), ())), precision=HIGH, preferred_element_type=F32)


def plan_part(target, source, valid, targets):
    count = target.shape[0]
    ids = jnp.arange(count, dtype=jnp.int32)
    key = jnp.where(valid, target, targets) * count + ids
    rank = jnp.sum((key[None, :] < key[:, None]).astype(jnp.int32), axis=1)
    place = rank[None, :] == ids[:, None]
    perm = jnp.sum(jnp.where(place, ids[None, :], 0), axis=1)
    sorted_target = jnp.sum(jnp.where(place, (key // count)[None, :], 0), axis=1)
    sorted_source = jnp.sum(jnp.where(place, jnp.where(valid, source, 0)[None, :], 0), axis=1)
    before = jnp.concatenate([jnp.full((1,), -1, jnp.int32), sorted_target[:-1]])
    keep = (before == sorted_target).astype(jnp.int32)
    span = jnp.arange(SLOTS, dtype=jnp.int32)
    upto = jnp.sum((key[None, :] < (span[:, None] + 1) * count).astype(jnp.int32), axis=1)
    some = jnp.sum((target[None, :] == span[:, None]) & valid[None, :], axis=1)
    last = jnp.where(some > 0, upto - 1, count)
    return [perm, keep, sorted_source, last]


def factor(m_ref):
    rows = lax.broadcasted_iota(jnp.int32, (64, 1), 0)

    def block(b, carry):
        mat, diag = carry
        live = rows < 64 - 8 * b
        for j in range(8):
            pivot = mat[j : j + 1, j : j + 1]
            below = live & (rows > j)
            scaled = jnp.where(below, mat[:, j : j + 1], 0.0) * (1.0 / pivot)
            diag = jnp.where(rows == j, pivot, diag)
            mat = mat - scaled * mat[j : j + 1, :]
        mat = pltpu.roll(mat, 120, 1)
        mat = jnp.concatenate([mat[8:], mat[:8]], axis=0)
        diag = jnp.concatenate([diag[8:], diag[:8]], axis=0)
        return mat, diag

    mat, diag = lax.fori_loop(0, 8, block, (m_ref[...], jnp.zeros((64, 1), F32)))
    mat = pltpu.roll(mat, 64, 1) * lax.rsqrt(diag)
    lanes = lax.broadcasted_iota(jnp.int32, (64, 128), 1)
    row = lax.broadcasted_iota(jnp.int32, (64, 128), 0)
    m_ref[...] = jnp.where((lanes >= 64) | (lanes >= row), mat, 0.0)


def kernel(
    plan, start_ref, blocks_ref, basis_ref, alpha_ref, beta_ref,
    q_ref, y_ref, r_ref, x_ref, m_ref, sums,
    ag_src, stripe_0, stripe_1, stripe_2, colset_0, colset_1, colset_2, pair_src, pair_dst, zed_src, zed_dst, row_src, row_dst,
    ar_src, ar1, ar_s1, ar2, ar_s2, ar3, ar_s3, ar4,
    op_send, op_recv, ar_send, ar_recv,
):
    r = lax.axis_index("row")
    c = lax.axis_index("col")
    z, k = r // 2, lax.rem(r, 2)
    cp, ch = lax.rem(c, 8), c // 8
    sibling = (z * 2 + (1 - k), c)

    def along_z(o):
        there = lax.rem(z + o, NZ)
        return there, (there * 2 + k, c)

    def along_c(o):
        there = lax.rem(c + o, NC)
        return there, (r, there)

    barrier = pltpu.get_barrier_semaphore()
    for o in range(1, 16):
        pl.semaphore_signal(barrier, inc=1, device_id=along_z(o)[1], device_id_type=MESH)
        pl.semaphore_signal(barrier, inc=1, device_id=along_c(o)[1], device_id_type=MESH)
    pl.semaphore_signal(barrier, inc=1, device_id=sibling, device_id_type=MESH)
    pl.semaphore_wait(barrier, 31)

    stripes = (stripe_0, stripe_1, stripe_2)
    colsets = (colset_0, colset_1, colset_2)

    def push(src, dst, send, recv, where):
        pltpu.make_async_remote_copy(
            src_ref=src, dst_ref=dst, send_sem=send, recv_sem=recv, device_id=where, device_id_type=MESH
        ).start()

    def settle(ref, sem):
        pltpu.make_async_copy(ref, ref, sem).wait()

    sums[SLOTS] = jnp.zeros((64, 128), F32)

    def reduce_1(s):
        ar_src[s] = x_ref[...].reshape(8, 8, 128)
        ar1[s, c] = ar_src[s, cp]
        for o in range(1, 16):
            there, where = along_c(o)
            push(ar_src.at[s, lax.rem(there, 8)], ar1.at[s, c], ar_send.at[s, 0], ar_recv.at[s, 0], where)

    def reduce_2(s):
        settle(ar1.at[s, pl.ds(0, 15)], ar_recv.at[s, 0])
        total = ar1[s, 0]
        for i in range(1, 16):
            total = total + ar1[s, i]
        ar_s1[s] = total
        push(ar_s1.at[s], ar2.at[s], ar_send.at[s, 1], ar_recv.at[s, 1], sibling)
        settle(ar2.at[s], ar_recv.at[s, 1])
        ar_s2[s] = ar_s1[s] + ar2[s]
        ar3[s, z] = ar_s2[s]
        for o in FAR:
            push(ar_s2.at[s], ar3.at[s, z], ar_send.at[s, 2], ar_recv.at[s, 2], along_z(o)[1])

    def reduce_3(s):
        settle(ar3.at[s, pl.ds(0, 15)], ar_recv.at[s, 2])
        total = ar3[s, 0]
        for i in range(1, 16):
            total = total + ar3[s, i]
        ar_s3[s] = total
        ar4[s, cp] = total
        for o in range(1, 8):
            there = ch * 8 + lax.rem(cp + o, 8)
            push(ar_s3.at[s], ar4.at[s, cp], ar_send.at[s, 3], ar_recv.at[s, 3], (r, there))

    def reduce_4(s):
        settle(ar4.at[s, pl.ds(0, 7)], ar_recv.at[s, 3])
        x_ref[...] = ar4[s].reshape(64, 128) * (1.0 / (512 * 128))

    def reduce_end(s):
        settle(ar1.at[s, pl.ds(0, 15)], ar_send.at[s, 0])
        settle(ar2.at[s], ar_send.at[s, 1])
        settle(ar3.at[s, pl.ds(0, 15)], ar_send.at[s, 2])
        settle(ar4.at[s, pl.ds(0, 7)], ar_send.at[s, 3])

    def spread(t, value):
        ag_src[t] = value.astype(BF16)
        stripes[t][c] = ag_src[t]
        colsets[t][k * 16 + z] = ag_src[t]
        row_dst[t, c] = jnp.zeros((64, 128), BF16)
        zed_dst[t, z] = jnp.zeros((64, 128), BF16)
        for o, p in zip(FAR, range(1, 16)):
            push(ag_src.at[t], colsets[t].at[k * 16 + z], op_send.at[t, 0], op_recv.at[t, 0], along_z(o)[1])
            push(ag_src.at[t], stripes[t].at[c], op_send.at[t, 1], op_recv.at[t, 1], along_c(p)[1])

    def products(base, source, transposed):
        dims = (((1,), (1,)), ((), ())) if transposed else (((1,), (0,)), ((), ()))

        def one(p, total):
            part = lax.dot_general(
                source[plan[base + 64 + p]], blocks_ref[plan[base + p]], dims, preferred_element_type=F32
            )
            total = jnp.where(plan[base + 32 + p] > 0, total, 0.0) + part
            sums[p] = total
            return total

        lax.fori_loop(0, SLOTS, one, jnp.zeros((64, 128), F32), unroll=8)

    def backward(t):
        settle(stripes[t].at[pl.ds(0, 15)], op_recv.at[t, 1])
        products(128, stripes[t], False)
        for i in range(NZ):
            pair_src[t, i] = sums[plan[224 + (1 - k) * 16 + i]].astype(BF16)
        push(pair_src.at[t], pair_dst.at[t], op_send.at[t, 2], op_recv.at[t, 2], sibling)
        settle(pair_dst.at[t], op_recv.at[t, 2])
        for o in FAR:
            there, where = along_z(o)
            zed_src[t, there] = (sums[plan[224 + k * 16 + there]] + pair_dst[t, there].astype(F32)).astype(BF16)
            push(zed_src.at[t, there], zed_dst.at[t, z], op_send.at[t, 3], op_recv.at[t, 3], where)
        return sums[plan[224 + k * 16 + z]] + pair_dst[t, z].astype(F32)

    def relay(t):
        settle(colsets[t].at[pl.ds(0, 15)], op_recv.at[t, 0])
        half = pl.ds(k * 16, 16)
        push(colsets[t].at[half], colsets[t].at[half], op_send.at[t, 4], op_recv.at[t, 4], sibling)
        settle(colsets[t].at[pl.ds(0, 16)], op_recv.at[t, 4])

    def forward(t):
        products(0, colsets[t], True)
        for o in range(1, 16):
            there, where = along_c(o)
            row_src[t, there] = sums[plan[96 + there]].astype(BF16)
            push(row_src.at[t, there], row_dst.at[t, c], op_send.at[t, 5], op_recv.at[t, 5], where)
        return sums[plan[96 + c]]

    def collect(t, own):
        settle(row_dst.at[t, pl.ds(0, 15)], op_recv.at[t, 5])
        total = own
        for i in range(NC):
            total = total + row_dst[t, i].astype(F32)
        settle(zed_dst.at[t, pl.ds(0, 15)], op_recv.at[t, 3])
        for i in range(NZ):
            total = total + zed_dst[t, i].astype(F32)
        return total

    def operator_end(t):
        settle(colsets[t].at[pl.ds(0, 15)], op_send.at[t, 0])
        settle(stripes[t].at[pl.ds(0, 15)], op_send.at[t, 1])
        settle(pair_dst.at[t], op_send.at[t, 2])
        settle(zed_dst.at[t, pl.ds(0, 15)], op_send.at[t, 3])
        settle(colsets[t].at[pl.ds(0, 16)], op_send.at[t, 4])
        settle(row_dst.at[t, pl.ds(0, 15)], op_send.at[t, 5])

    lanes = lax.broadcasted_iota(jnp.int32, (64, 64), 1)
    rows = lax.broadcasted_iota(jnp.int32, (64, 64), 0)
    eye = (lanes == rows).astype(F32)

    def factor_start():
        m_ref[:, 0:64] = x_ref[:, 0:64]
        m_ref[:, 64:128] = eye
        factor(m_ref)

    def factor_step(t):
        alpha_t = x_ref[:, 64:128]
        alpha_ref[t] = alpha_t
        m_ref[:, 0:64] = x_ref[:, 0:64] - nt(alpha_t, alpha_t)
        m_ref[:, 64:128] = eye
        factor(m_ref)
        beta_ref[t] = m_ref[:, 0:64]
        return alpha_t

    first = start_ref[...]
    x_ref[...] = nt(first, jnp.concatenate([first, first], axis=0))
    reduce_1(0)
    reduce_2(0)
    reduce_3(0)
    reduce_4(0)
    factor_start()
    q_ref[...] = nn(m_ref[:, 64:128], first)
    spread(0, q_ref[...])
    own = backward(0)
    relay(0)
    own = own + forward(0)
    reduce_end(0)
    y_ref[...] = collect(0, own)
    r_ref[...] = y_ref[...]
    operator_end(0)

    def gram(s):
        x_ref[...] = nt(r_ref[...], jnp.concatenate([r_ref[...], q_ref[...]], axis=0))
        reduce_1(s)

    def step(s):
        spread(s, r_ref[...])
        gram(s)
        own = backward(s)
        reduce_2(s)
        relay(s)
        own = own + forward(s)
        reduce_3(s)
        reduce_4(s)
        alpha_t = factor_step(s - 1)
        inverse = m_ref[:, 64:128]
        following = nn(inverse, r_ref[...] - nn(alpha_t, q_ref[...]))
        reduce_end(s)
        image = collect(s, own)
        y_ref[...] = nn(inverse, image - nn(alpha_t, y_ref[...]))
        r_ref[...] = y_ref[...] - nn(m_ref[:, 0:64], q_ref[...])
        q_ref[...] = following
        operator_end(s)

    for s in range(1, ITERS):
        step(s)
    gram(ITERS)
    reduce_2(ITERS)
    reduce_3(ITERS)
    reduce_4(ITERS)
    alpha_t = factor_step(ITERS - 1)
    basis_ref[...] = nn(m_ref[:, 64:128], r_ref[...] - nn(alpha_t, q_ref[...]))
    reduce_end(ITERS)


def shards(blocks, block_rows, block_cols, start):
    row_index = lax.axis_index("row")
    valid = block_rows < 512
    row_target = block_rows - row_index * NC
    col_owner = block_cols // NC
    col_target = lax.rem(col_owner, 2) * NZ + col_owner // 2
    plan = jnp.concatenate(
        plan_part(row_target, col_target, valid, NC) + plan_part(col_target, row_target, valid, 2 * NZ)
    )
    vmem = pl.BlockSpec(memory_space=pltpu.VMEM)
    wide = (ITERS, 16, 64, 128)
    tall = (ITERS + 1, 16, 8, 128)
    piece = (ITERS + 1, 8, 128)
    basis, alphas, betas = pl.pallas_call(
        kernel,
        out_shape=(
            jax.ShapeDtypeStruct((64, 128), F32),
            jax.ShapeDtypeStruct((ITERS, 64, 64), F32),
            jax.ShapeDtypeStruct((ITERS, 64, 64), F32),
        ),
        in_specs=[pl.BlockSpec(memory_space=pltpu.SMEM), vmem, vmem],
        out_specs=(vmem, vmem, vmem),
        scratch_shapes=[
            pltpu.VMEM((64, 128), F32),
            pltpu.VMEM((64, 128), F32),
            pltpu.VMEM((64, 128), F32),
            pltpu.VMEM((64, 128), F32),
            pltpu.VMEM((64, 128), F32),
            pltpu.VMEM((SLOTS + 1, 64, 128), F32),
            pltpu.VMEM((ITERS, 64, 128), BF16),
            pltpu.VMEM(wide[1:], BF16),
            pltpu.VMEM(wide[1:], BF16),
            pltpu.VMEM(wide[1:], BF16),
            pltpu.VMEM((32, 64, 128), BF16),
            pltpu.VMEM((32, 64, 128), BF16),
            pltpu.VMEM((32, 64, 128), BF16),
            pltpu.VMEM(wide, BF16),
            pltpu.VMEM(wide, BF16),
            pltpu.VMEM(wide, BF16),
            pltpu.VMEM(wide, BF16),
            pltpu.VMEM(wide, BF16),
            pltpu.VMEM(wide, BF16),
            pltpu.VMEM((ITERS + 1, 8, 8, 128), F32),
            pltpu.VMEM(tall, F32),
            pltpu.VMEM(piece, F32),
            pltpu.VMEM(piece, F32),
            pltpu.VMEM(piece, F32),
            pltpu.VMEM(tall, F32),
            pltpu.VMEM(piece, F32),
            pltpu.VMEM((ITERS + 1, 8, 8, 128), F32),
            pltpu.SemaphoreType.DMA((ITERS, 6)),
            pltpu.SemaphoreType.DMA((ITERS, 6)),
            pltpu.SemaphoreType.DMA((ITERS + 1, 4)),
            pltpu.SemaphoreType.DMA((ITERS + 1, 4)),
        ],
        compiler_params=pltpu.CompilerParams(collective_id=0, has_side_effects=True, vmem_limit_bytes=36 << 20),
        name="lanczos",
    )(plan, start, blocks)
    return (basis, jnp.swapaxes(alphas, 1, 2), jnp.swapaxes(betas, 1, 2))


def solution(mesh):
    in_specs = (
        P(("row", "col"), None, None),
        P(("row", "col")),
        P(("row", "col")),
        P(None, ("row", "col")),
    )
    out_specs = (P(None, ("row", "col")), P(), P())
    return jax.shard_map(shards, mesh=mesh, in_specs=in_specs, out_specs=out_specs, check_vma=False)
```

time: 1520 us -> 176 us (0.12)
  blocking collectives: 872 us -> 0 us
  waiting for transfers between devices: 548 us -> 0 us
  Pallas kernels: 0 us -> 169 us
  other arithmetic: 49 us -> 0.77 us
  matrix products: 21.6 us -> 0 us
    psum x7 -> x0, blocking collectives: 727 us -> none  [the longest x3 319 us: shards(): alpha = lax.psum(local_inner(basis, residue), ('row', 'col')) / columns_all]
    reduce_scatter x3 -> x0, waiting for transfers between devices: 325 us -> none  [shards(): lax.psum_scatter(col_part.astype(jnp.bfloat16), 'row', scatter_dimension=...]
    unnamed x9 -> x0, waiting for transfers between devices: 223 us -> none
    pallas_call x0 -> x1, Pallas kernels: none -> 169 us  [shards(): pl.pallas_call(kernel, out_shape=(jax.ShapeDtypeStruct((64, 128), F32), j...]
    all_gather x6 -> x0, blocking collectives: 145 us -> none  [the longest x3 93.6 us: shards(): lax.all_gather(rounded, 'row', axis=1, tiled=True)]
    another operation x25 -> x0, other arithmetic: 48.9 us -> none  [the longest x12 26.1 us: factorize(): factor_low = jnp.linalg.cholesky(gramian)]
    dot_general x34 -> x0, matrix products: 20.6 us -> none  [the longest x3 3.84 us: shards(): jnp.einsum('ksd,sm->kmd', backward, hot_cols.astype(jnp.float32), precisi...]
  transfers between devices with their start and end apart: 6 -> 0, of which waited for: 6 -> 0; matrix products, arithmetic and copies ran while one was open for 1% -> 0% of each run, Pallas kernels for 0% -> 0%
where the time goes in v1:
time: 176 us
  Pallas kernels  169 us (96%)
  local copies, waits for them, and re-layouts  4.71 us (3%)
    pallas_call x1, Pallas kernels, shards(): pl.pallas_call(kernel, out_shape=(jax.ShapeDtypeStruct((64, 128), F32), j...  169 us
    unnamed x11, local copies, waits for them, and re-layouts  4.63 us

profile of v1, /device:TPU:1, one launch (start us, length us, event | category | flops | bytes accessed | tf_op | source)
XLA Modules:
  0.0 175.5 jit_solution(11498301842846859879)
XLA Ops:
  0.6 0.0 copy-start.2
  0.6 0.6 copy-done.2
  1.3 0.0 copy-start.3
  1.3 0.6 copy-done.3
  2.0 0.0 copy-start.1
  2.0 0.3 convert_reduce_fusion
  2.3 0.1 select_reduce_fusion.3
  2.4 0.1 compare_convert_fusion.1
  2.5 0.2 select_reduce_fusion
  2.7 0.1 compare_convert_fusion
  2.7 0.1 concatenate.11.plan
  2.8 0.0 copy-done.1
  2.8 0.0 copy-start
  2.8 1.2 copy-done
  4.1 169.3 %lanczos.1 = (f32[64,128]{1,0:T(8,128)S(1)}, f32[3,64,64]{2,1,0:T(8,128)S(1)}, f32[3,64,64]{2,1,0:T(8,128)S(1)}) custom-call(s32[256]{0:T(256)S(1)} %concatenate.11.plan, f32[64,128]{1,0:T(8,128)S(1)} %copy-done.1, bf16[32,128,128]{2,1,0:T(8,128)(2,1)S(1)} %copy-done), custom_call_target="tpu_custom_call" | custom-call | tf_op jit(solution)/shard_map/lanczos/pallas_call | solution.py:302
  173.4 0.7 copy.9
  174.2 0.7 copy.10
  174.9 0.6 copy.12
  (6 shorter events, 0.1 us)
Async XLA Ops:
  0.6 0.7 copy-start.2
  1.3 0.7 copy-start.3
  2.0 0.8 copy-start.1
  2.8 1.2 copy-start

commit v2 on v1

v2 whole, which is shorter than its diff:
```python
import jax
import jax.numpy as jnp
from jax import lax
from jax.experimental import pallas as pl
from jax.experimental.pallas import tpu as pltpu
from jax.sharding import PartitionSpec as P

ITERS = 3
HIGH = lax.Precision.HIGHEST
MESH = pl.DeviceIdType.MESH
F32 = jnp.float32
BF16 = jnp.bfloat16

NZ = 16
NC = 16
SLOTS = 32
REACH = (0, 3, 13, 6, 10, 8, 15, 2, 12, 5, 9, 1, 4, 14, 7, 11)
FAR = (8, 7, 9, 6, 10, 5, 11, 4, 12, 3, 13, 2, 14, 1, 15)


def nt(a, b):
    return lax.dot_general(a, b, (((1,), (1,)), ((), ())), precision=HIGH, preferred_element_type=F32)


def nn(a, b):
    return lax.dot_general(a, b, (((1,), (0,)), ((), ())), precision=HIGH, preferred_element_type=F32)


def plan_part(target, source, valid, targets):
    count = target.shape[0]
    ids = jnp.arange(count, dtype=jnp.int32)
    key = jnp.where(valid, target, targets) * count + ids
    rank = jnp.sum((key[None, :] < key[:, None]).astype(jnp.int32), axis=1)
    place = rank[None, :] == ids[:, None]
    perm = jnp.sum(jnp.where(place, ids[None, :], 0), axis=1)
    sorted_target = jnp.sum(jnp.where(place, (key // count)[None, :], 0), axis=1)
    sorted_source = jnp.sum(jnp.where(place, jnp.where(valid, source, 0)[None, :], 0), axis=1)
    before = jnp.concatenate([jnp.full((1,), -1, jnp.int32), sorted_target[:-1]])
    keep = (before == sorted_target).astype(jnp.int32)
    span = jnp.arange(SLOTS, dtype=jnp.int32)
    upto = jnp.sum((key[None, :] < (span[:, None] + 1) * count).astype(jnp.int32), axis=1)
    some = jnp.sum((target[None, :] == span[:, None]) & valid[None, :], axis=1)
    last = jnp.where(some > 0, upto - 1, count)
    return [perm, keep, sorted_source, last]


def factor(m_ref):
    rest = m_ref[...]
    done = []
    for b in range(8):
        shape = rest.shape
        row = lax.broadcasted_iota(jnp.int32, shape, 0)
        cols = [jnp.broadcast_to(rest[:, 8 * b + i : 8 * b + i + 1], shape) for i in range(8)]
        for j in range(0, 8, 2):
            c0, c1 = cols[j], cols[j + 1]
            one, off, two = c0[j : j + 1], c0[j + 1 : j + 2], c1[j + 1 : j + 2]
            inv0 = 1.0 / one
            inv1 = one * (1.0 / (one * two - off * off))
            share = off * inv0
            r0 = rest[j : j + 1]
            r1 = rest[j + 1 : j + 2] - share * r0
            c1 = c1 - share * c0
            for i in range(j + 2, 8):
                cols[i] = cols[i] - c0 * (c0[i : i + 1] * inv0) - c1 * (c1[i : i + 1] * inv1)
            low = row > j + 1
            new = rest - jnp.where(low, c0, 0.0) * (inv0 * r0) - jnp.where(low, c1, 0.0) * (inv1 * r1)
            rest = jnp.where(row == j + 1, jnp.broadcast_to(r1, shape), new)
        done.append(rest[:8])
        rest = rest[8:]
    mat = jnp.concatenate(done, axis=0)
    lanes = lax.broadcasted_iota(jnp.int32, (64, 128), 1)
    row = lax.broadcasted_iota(jnp.int32, (64, 128), 0)
    diag = jnp.sum(jnp.where(lanes == row, mat, 0.0), axis=1, keepdims=True)
    m_ref[...] = jnp.where((lanes >= 64) | (lanes >= row), mat * lax.rsqrt(diag), 0.0)


def kernel(
    plan, start_ref, blocks_ref, basis_ref, alpha_ref, beta_ref,
    q_ref, y_ref, r_ref, x_ref, m_ref, sums, held, buffers,
    ar_src, ar1, ar_s1, ar2, ar_s2, ar3, ar_s3, ar4, ar_send, ar_recv,
):
    r = lax.axis_index("row")
    c = lax.axis_index("col")
    z, k = r // 2, lax.rem(r, 2)
    cp, ch = lax.rem(c, 8), c // 8
    sibling = (z * 2 + (1 - k), c)
    mine, other = k * 16, (1 - k) * 16

    def along_z(o):
        there = lax.rem(z + o + NZ, NZ)
        return there, (there * 2 + k, c)

    def along_c(o):
        there = lax.rem(c + o, NC)
        return there, (r, there)

    barrier = pltpu.get_barrier_semaphore()
    for o in range(1, 16):
        pl.semaphore_signal(barrier, inc=1, device_id=along_z(o)[1], device_id_type=MESH)
        pl.semaphore_signal(barrier, inc=1, device_id=along_c(o)[1], device_id_type=MESH)
    pl.semaphore_signal(barrier, inc=1, device_id=sibling, device_id_type=MESH)

    def push(src, dst, send, recv, where):
        pltpu.make_async_remote_copy(
            src_ref=src, dst_ref=dst, send_sem=send, recv_sem=recv, device_id=where, device_id_type=MESH
        ).start()

    def settle(ref, sem):
        pltpu.make_async_copy(ref, ref, sem).wait()

    def reduce_1(s):
        ar_src[s] = x_ref[...].reshape(8, 8, 128)
        ar1[s, c] = ar_src[s, cp]
        for o in range(1, 16):
            there, where = along_c(o)
            push(ar_src.at[s, lax.rem(there, 8)], ar1.at[s, c], ar_send.at[s, 0], ar_recv.at[s, 0], where)

    def reduce_2(s):
        settle(ar1.at[s, pl.ds(0, 15)], ar_recv.at[s, 0])
        total = ar1[s, 0]
        for i in range(1, 16):
            total = total + ar1[s, i]
        ar_s1[s] = total
        push(ar_s1.at[s], ar2.at[s], ar_send.at[s, 1], ar_recv.at[s, 1], sibling)

    def reduce_3(s):
        settle(ar2.at[s], ar_recv.at[s, 1])
        ar_s2[s] = ar_s1[s] + ar2[s]
        ar3[s, z] = ar_s2[s]
        for o in FAR:
            push(ar_s2.at[s], ar3.at[s, z], ar_send.at[s, 2], ar_recv.at[s, 2], along_z(o)[1])

    def reduce_4(s):
        settle(ar3.at[s, pl.ds(0, 15)], ar_recv.at[s, 2])
        total = ar3[s, 0]
        for i in range(1, 16):
            total = total + ar3[s, i]
        ar_s3[s] = total
        ar4[s, cp] = total
        for o in range(1, 8):
            there = ch * 8 + lax.rem(cp + o, 8)
            push(ar_s3.at[s], ar4.at[s, cp], ar_send.at[s, 3], ar_recv.at[s, 3], (r, there))

    def reduce_5(s):
        settle(ar4.at[s, pl.ds(0, 7)], ar_recv.at[s, 3])
        x_ref[...] = ar4[s].reshape(64, 128) * (1.0 / (512 * 128))

    def reduce_end(s):
        settle(ar1.at[s, pl.ds(0, 15)], ar_send.at[s, 0])
        settle(ar2.at[s], ar_send.at[s, 1])
        settle(ar3.at[s, pl.ds(0, 15)], ar_send.at[s, 2])
        settle(ar4.at[s, pl.ds(0, 7)], ar_send.at[s, 3])

    def spread(t, value):
        u = buffers[t]
        value = value.astype(u["src"].dtype)
        u["src"][...] = value
        u["stripe"][c] = value
        u["colset"][mine] = value
        u["row_dst"][c] = jnp.zeros_like(value)
        for o, slot in ((6, 4), (-6, 3), (3, 2), (-3, 1)):
            sem = u["recv"].at[1 if slot > 2 else 0]
            push(u["src"], u["colset"].at[mine + slot], u["send"].at[0], sem, along_z(o)[1])
        push(u["src"], u["colset"].at[mine + 6], u["send"].at[0], u["recv"].at[2], along_z(1)[1])
        push(u["src"], u["colset"].at[mine + 11], u["send"].at[0], u["recv"].at[2], along_z(-1)[1])
        push(u["src"], u["colset"].at[mine + 5], u["send"].at[0], u["recv"].at[2], along_z(8)[1])
        for o in range(1, 16):
            push(u["src"], u["stripe"].at[c], u["send"].at[3], u["recv"].at[3], along_c(o)[1])

    def hop(t, first):
        u = buffers[t]
        settle(u["colset"].at[pl.ds(0, 2)], u["recv"].at[0 if first == 1 else 1])
        source = u["colset"].at[pl.ds(mine + first, 2)]
        for o, base in ((1, 6), (-1, 11)):
            target = u["colset"].at[pl.ds(mine + base + first, 2)]
            push(source, target, u["send"].at[0], u["recv"].at[2], along_z(o)[1])

    def relay(t, first, count):
        u = buffers[t]
        part = u["colset"].at[pl.ds(mine + first, count)]
        push(part, part, u["send"].at[4], u["recv"].at[4], sibling)

    def products(base, source, transposed):
        dims = (((1,), (1,)), ((), ())) if transposed else (((1,), (0,)), ((), ()))

        def one(p, total):
            value = source[plan[base + 64 + p]]
            matrix = blocks_ref[plan[base + p]]
            high = value.astype(BF16)
            part = lax.dot_general(high, matrix, dims, preferred_element_type=F32)
            if value.dtype == F32:
                low = (value - high.astype(F32)).astype(BF16)
                part = part + lax.dot_general(low, matrix, dims, preferred_element_type=F32)
            total = jnp.where(plan[base + 32 + p] > 0, total, 0.0) + part
            sums[p] = total
            return total

        lax.fori_loop(0, SLOTS, one, jnp.zeros((64, 128), F32), unroll=8)

    def backward(t):
        u = buffers[t]
        kind = u["src"].dtype
        settle(u["stripe"].at[pl.ds(0, 15)], u["recv"].at[3])
        products(128, u["stripe"], False)
        for i in range(NZ):
            u["pair_src"][i] = sums[plan[224 + other + i]].astype(kind)
        push(u["pair_src"], u["pair_dst"], u["send"].at[5], u["recv"].at[5], sibling)
        settle(u["pair_dst"], u["recv"].at[5])
        for i in range(15, 4, -1):
            u["zed_src"][i] = (sums[plan[224 + mine + i]] + u["pair_dst"][i].astype(F32)).astype(kind)
            if i == 11:
                push(u["zed_src"].at[pl.ds(11, 5)], u["near"].at[pl.ds(0, 5)], u["send"].at[6], u["recv"].at[6], along_z(1)[1])
            if i == 6:
                push(u["zed_src"].at[pl.ds(6, 5)], u["near"].at[pl.ds(5, 5)], u["send"].at[6], u["recv"].at[6], along_z(-1)[1])
        push(u["zed_src"].at[5], u["far"].at[4], u["send"].at[7], u["recv"].at[7], along_z(8)[1])
        for i in range(5):
            held[i] = sums[plan[224 + mine + i]] + u["pair_dst"][i].astype(F32)

    def forward(t):
        u = buffers[t]
        settle(u["colset"].at[pl.ds(0, 16)], u["recv"].at[4])
        products(0, u["colset"], True)
        for o in range(1, 16):
            there, where = along_c(o)
            u["row_src"][there] = sums[plan[96 + there]].astype(u["src"].dtype)
            push(u["row_src"].at[there], u["row_dst"].at[c], u["send"].at[8], u["recv"].at[8], where)

    def pass_on(t):
        u = buffers[t]
        settle(u["near"], u["recv"].at[6])
        for i, o in ((3, 6), (4, -6), (1, 3), (2, -3)):
            total = held[i] + u["near"][i].astype(F32) + u["near"][5 + i].astype(F32)
            u["zed_src"][i] = total.astype(u["src"].dtype)
            push(u["zed_src"].at[i], u["far"].at[i - 1], u["send"].at[7], u["recv"].at[7], along_z(o)[1])

    def collect(t):
        u = buffers[t]
        total = held[0] + u["near"][0].astype(F32) + u["near"][5].astype(F32) + sums[plan[96 + c]]
        settle(u["row_dst"].at[pl.ds(0, 15)], u["recv"].at[8])
        for i in range(NC):
            total = total + u["row_dst"][i].astype(F32)
        settle(u["far"], u["recv"].at[7])
        for i in range(5):
            total = total + u["far"][i].astype(F32)
        return total

    def operator_end(t):
        u = buffers[t]
        settle(u["colset"].at[pl.ds(0, 15)], u["send"].at[0])
        settle(u["stripe"].at[pl.ds(0, 15)], u["send"].at[3])
        settle(u["colset"].at[pl.ds(0, 16)], u["send"].at[4])
        settle(u["pair_dst"], u["send"].at[5])
        settle(u["near"], u["send"].at[6])
        settle(u["far"], u["send"].at[7])
        settle(u["row_dst"].at[pl.ds(0, 15)], u["send"].at[8])

    lanes = lax.broadcasted_iota(jnp.int32, (64, 64), 1)
    rows = lax.broadcasted_iota(jnp.int32, (64, 64), 0)
    eye = (lanes == rows).astype(F32)

    def factor_start():
        m_ref[:, 0:64] = x_ref[:, 0:64]
        m_ref[:, 64:128] = eye
        factor(m_ref)

    def factor_step(t):
        alpha_t = x_ref[:, 64:128]
        alpha_ref[t] = alpha_t
        m_ref[:, 0:64] = x_ref[:, 0:64] - nt(alpha_t, alpha_t)
        m_ref[:, 64:128] = eye
        factor(m_ref)
        beta_ref[t] = m_ref[:, 0:64]
        return alpha_t

    sums[SLOTS] = jnp.zeros((64, 128), F32)
    first = start_ref[...]
    x_ref[...] = nt(first, jnp.concatenate([first, first], axis=0))
    pl.semaphore_wait(barrier, 31)

    for s in range(ITERS):
        if s:
            x_ref[...] = nt(r_ref[...], jnp.concatenate([r_ref[...], q_ref[...]], axis=0))
        reduce_1(s)
        spread(s, r_ref[...] if s else first)
        hop(s, 1)
        reduce_2(s)
        hop(s, 3)
        relay(s, 0, 5)
        reduce_3(s)
        backward(s)
        settle(buffers[s]["colset"].at[pl.ds(0, 11)], buffers[s]["recv"].at[2])
        relay(s, 5, 11)
        forward(s)
        pass_on(s)
        reduce_4(s)
        reduce_5(s)
        if s == 0:
            factor_start()
            inverse = m_ref[:, 64:128]
            q_ref[...] = nn(inverse, first)
            y_ref[...] = nn(inverse, collect(s))
            r_ref[...] = y_ref[...]
        else:
            alpha_t = factor_step(s - 1)
            inverse = m_ref[:, 64:128]
            following = nn(inverse, r_ref[...] - nn(alpha_t, q_ref[...]))
            less = nn(alpha_t, y_ref[...])
            carried = nn(m_ref[:, 0:64], q_ref[...])
            y_ref[...] = nn(inverse, collect(s) - less)
            r_ref[...] = y_ref[...] - carried
            q_ref[...] = following
    x_ref[...] = nt(r_ref[...], jnp.concatenate([r_ref[...], q_ref[...]], axis=0))
    reduce_1(ITERS)
    for s in range(ITERS):
        operator_end(s)
        reduce_end(s)
    reduce_2(ITERS)
    reduce_3(ITERS)
    reduce_4(ITERS)
    reduce_5(ITERS)
    alpha_t = factor_step(ITERS - 1)
    basis_ref[...] = nn(m_ref[:, 64:128], r_ref[...] - nn(alpha_t, q_ref[...]))
    reduce_end(ITERS)


def shards(blocks, block_rows, block_cols, start):
    row_index = lax.axis_index("row")
    valid = block_rows < 512
    row_target = block_rows - row_index * NC
    col_owner = block_cols // NC
    away = lax.rem(col_owner // 2 - row_index // 2 + 3 * NZ, NZ)
    slot = jnp.sum(jnp.where(away[:, None] == jnp.array(REACH)[None, :], jnp.arange(NZ)[None, :], 0), axis=1)
    col_target = lax.rem(col_owner, 2) * NZ + slot
    plan = jnp.concatenate(
        plan_part(row_target, col_target, valid, NC) + plan_part(col_target, row_target, valid, 2 * NZ)
    )
    vmem = pl.BlockSpec(memory_space=pltpu.VMEM)
    tall = (ITERS + 1, 16, 8, 128)
    piece = (ITERS + 1, 8, 128)

    def buffer(kind):
        counts = dict(
            stripe=16, colset=32, pair_src=16, pair_dst=16, zed_src=16, near=10, far=5, row_src=16, row_dst=16
        )
        made = {name: pltpu.VMEM((count, 64, 128), kind) for name, count in counts.items()}
        made["src"] = pltpu.VMEM((64, 128), kind)
        made["send"] = pltpu.SemaphoreType.DMA((9,))
        made["recv"] = pltpu.SemaphoreType.DMA((9,))
        return made

    basis, alphas, betas = pl.pallas_call(
        kernel,
        out_shape=(
            jax.ShapeDtypeStruct((64, 128), F32),
            jax.ShapeDtypeStruct((ITERS, 64, 64), F32),
            jax.ShapeDtypeStruct((ITERS, 64, 64), F32),
        ),
        in_specs=[pl.BlockSpec(memory_space=pltpu.SMEM), vmem, vmem],
        out_specs=(vmem, vmem, vmem),
        scratch_shapes=[
            pltpu.VMEM((64, 128), F32),
            pltpu.VMEM((64, 128), F32),
            pltpu.VMEM((64, 128), F32),
            pltpu.VMEM((64, 128), F32),
            pltpu.VMEM((64, 128), F32),
            pltpu.VMEM((SLOTS + 1, 64, 128), F32),
            pltpu.VMEM((5, 64, 128), F32),
            [buffer(F32), buffer(BF16), buffer(BF16)],
            pltpu.VMEM((ITERS + 1, 8, 8, 128), F32),
            pltpu.VMEM(tall, F32),
            pltpu.VMEM(piece, F32),
            pltpu.VMEM(piece, F32),
            pltpu.VMEM(piece, F32),
            pltpu.VMEM(tall, F32),
            pltpu.VMEM(piece, F32),
            pltpu.VMEM((ITERS + 1, 8, 8, 128), F32),
            pltpu.SemaphoreType.DMA((ITERS + 1, 4)),
            pltpu.SemaphoreType.DMA((ITERS + 1, 4)),
        ],
        compiler_params=pltpu.CompilerParams(collective_id=0, has_side_effects=True, vmem_limit_bytes=36 << 20),
        name="lanczos",
    )(plan, start, blocks)
    return (basis, jnp.swapaxes(alphas, 1, 2), jnp.swapaxes(betas, 1, 2))


def solution(mesh):
    in_specs = (
        P(("row", "col"), None, None),
        P(("row", "col")),
        P(("row", "col")),
        P(None, ("row", "col")),
    )
    out_specs = (P(None, ("row", "col")), P(), P())
    return jax.shard_map(shards, mesh=mesh, in_specs=in_specs, out_specs=out_specs, check_vma=False)
```

time: 176 us -> 123 us (0.70)
  Pallas kernels: 169 us -> 116 us
    pallas_call x1, Pallas kernels: 169 us -> 116 us  [shards(): pl.pallas_call(kernel, out_shape=(jax.ShapeDtypeStruct((64, 128), F32), j...]
    unnamed x11 -> x13, local copies, waits for them, and re-layouts: 4.63 us -> 5.28 us
where the time goes in v2:
time: 123 us
  Pallas kernels  116 us (94%)
  local copies, waits for them, and re-layouts  5.36 us (4%)
    pallas_call x1, Pallas kernels, shards(): pl.pallas_call(kernel, out_shape=(jax.ShapeDtypeStruct((64, 128), F32), j...  116 us
    unnamed x13, local copies, waits for them, and re-layouts  5.28 us

profile of v2, /device:TPU:1, one launch (start us, length us, event | category | flops | bytes accessed | tf_op | source)
XLA Modules:
  0.0 122.5 jit_solution(4902967328809062822)
XLA Ops:
  0.6 0.0 copy-start.2
  0.7 0.6 copy-done.2
  1.3 0.0 copy-start.3
  1.3 0.6 copy-done.3
  2.0 0.0 copy-start.4
  2.0 0.6 copy-done.4
  2.6 0.1 select_reduce_fusion.6
  2.8 0.0 copy-start.1
  2.8 0.3 convert_reduce_fusion
  3.1 0.1 select_reduce_fusion.3
  3.2 0.1 compare_convert_fusion.1
  3.3 0.2 select_reduce_fusion
  3.4 0.1 compare_convert_fusion
  3.5 0.1 concatenate.11.plan
  3.6 0.0 copy-done.1
  3.6 0.0 copy-start
  3.6 1.2 %copy-done = bf16[32,128,128]{2,1,0:T(8,128)(2,1)S(1)} copy-done((bf16[32,128,128]{2,1,0:T(8,128)(2,1)S(1)}, bf16[32,128,128]{2,1,0:T(8,128)(2,1)}, u32[]{:S(2)}) %copy-start) | copy-done | bytes 1048600
  4.8 115.6 %lanczos.1 = (f32[64,128]{1,0:T(8,128)S(1)}, f32[3,64,64]{2,1,0:T(8,128)S(1)}, f32[3,64,64]{2,1,0:T(8,128)S(1)}) custom-call(s32[256]{0:T(256)S(1)} %concatenate.11.plan, f32[64,128]{1,0:T(8,128)S(1)} %copy-done.1, bf16[32,128,128]{2,1,0:T(8,128)(2,1)S(1)} %copy-done), custom_call_target="tpu_custom_call" | custom-call | tf_op jit(solution)/shard_map/lanczos/pallas_call | solution.py:351
  120.4 0.7 copy.10
  121.2 0.7 copy.11
  121.9 0.6 copy.13
  (7 shorter events, 0.1 us)
Async XLA Ops:
  0.6 0.7 copy-start.2
  1.3 0.7 copy-start.3
  2.0 0.7 copy-start.4
  2.8 0.8 copy-start.1
  3.6 1.2 %copy-start = (bf16[32,128,128]{2,1,0:T(8,128)(2,1)S(1)}, bf16[32,128,128]{2,1,0:T(8,128)(2,1)}, u32[]{:S(2)}) copy-start(bf16[32,128,128]{2,1,0:T(8,128)(2,1)} %blocks_ref.1) | copy-start | bytes 3145732

commit v3 on v2

--- a/solution.py
+++ b/solution.py
@@ -14,6 +14,7 @@
 NZ = 16
 NC = 16
 SLOTS = 32
+HBM = pl.BlockSpec(memory_space=pltpu.HBM)
 REACH = (0, 3, 13, 6, 10, 8, 15, 2, 12, 5, 9, 1, 4, 14, 7, 11)
 FAR = (8, 7, 9, 6, 10, 5, 11, 4, 12, 3, 13, 2, 14, 1, 15)
 
@@ -27,21 +28,50 @@
 
 
 def plan_part(target, source, valid, targets):
-    count = target.shape[0]
-    ids = jnp.arange(count, dtype=jnp.int32)
-    key = jnp.where(valid, target, targets) * count + ids
-    rank = jnp.sum((key[None, :] < key[:, None]).astype(jnp.int32), axis=1)
-    place = rank[None, :] == ids[:, None]
-    perm = jnp.sum(jnp.where(place, ids[None, :], 0), axis=1)
-    sorted_target = jnp.sum(jnp.where(place, (key // count)[None, :], 0), axis=1)
-    sorted_source = jnp.sum(jnp.where(place, jnp.where(valid, source, 0)[None, :], 0), axis=1)
-    before = jnp.concatenate([jnp.full((1,), -1, jnp.int32), sorted_target[:-1]])
-    keep = (before == sorted_target).astype(jnp.int32)
-    span = jnp.arange(SLOTS, dtype=jnp.int32)
-    upto = jnp.sum((key[None, :] < (span[:, None] + 1) * count).astype(jnp.int32), axis=1)
-    some = jnp.sum((target[None, :] == span[:, None]) & valid[None, :], axis=1)
-    last = jnp.where(some > 0, upto - 1, count)
-    return [perm, keep, sorted_source, last]
+    across = lax.broadcasted_iota(jnp.int32, (SLOTS, SLOTS), 1).astype(F32)
+    down = lax.broadcasted_iota(jnp.int32, (SLOTS, SLOTS), 0).astype(F32)
+    diagonal = across == down
+
+    def upright(row):
+        return jnp.sum(jnp.where(diagonal, row, 0.0), axis=1, keepdims=True)
+
+    target = jnp.where(valid, target, float(targets))
+    key = target * SLOTS + across[:1]
+    key_down, target_down = upright(key), upright(target)
+    source_down = upright(jnp.where(valid, source, 0.0))
+    rank = jnp.sum(jnp.where(key < key_down, 1.0, 0.0), axis=1, keepdims=True)
+
+    def pick(column, place):
+        return jnp.sum(jnp.where(place, column, 0.0), axis=0, keepdims=True)
+
+    here = rank == across
+    one = jnp.ones_like(rank)
+    same = pick(target_down + 1.0, here) == pick(target_down + 1.0, rank + 1.0 == across)
+    upto = pick(one, key_down < (across + 1.0) * SLOTS)
+    some = pick(one, target_down == across)
+    last = jnp.where(some > 0.0, upto - 1.0, float(SLOTS))
+    rows = (pick(down[:, :1], here), jnp.where(same, 1.0, 0.0), pick(source_down, here), last)
+    return [row.astype(jnp.int32) for row in rows]
+
+
+def make_plan(rows_ref, cols_ref, plan_ref):
+    r = lax.axis_index("row")
+    z = r // 2
+    row_index, col_index = rows_ref[...], cols_ref[...]
+    valid = row_index < 512
+    owner = lax.shift_right_logical(col_index, 4)
+    away = (lax.shift_right_logical(owner, 1) - z + NZ) & 15
+    slot = jnp.zeros_like(away)
+    for i in range(1, NZ):
+        slot = jnp.where(away == REACH[i], i, slot)
+    row_target = jnp.clip(row_index - r * NC, 0, NC - 1).astype(F32)
+    col_target = ((owner & 1) * NZ + slot).astype(F32)
+    for base, part in (
+        (0, plan_part(row_target, col_target, valid, SLOTS)),
+        (4, plan_part(col_target, row_target, valid, SLOTS)),
+    ):
+        for i in range(4):
+            plan_ref[base + i : base + i + 1, 0:SLOTS] = part[i]
 
 
 def factor(m_ref):
@@ -75,8 +105,8 @@
 
 
 def kernel(
-    plan, start_ref, blocks_ref, basis_ref, alpha_ref, beta_ref,
-    q_ref, y_ref, r_ref, x_ref, m_ref, sums, held, buffers,
+    plan, start_hbm, blocks_hbm, basis_ref, alpha_ref, beta_ref,
+    start_ref, blocks_ref, copy_sem, q_ref, y_ref, r_ref, x_ref, m_ref, sums, held, buffers,
     ar_src, ar1, ar_s1, ar2, ar_s2, ar3, ar_s3, ar4, ar_send, ar_recv,
 ):
     r = lax.axis_index("row")
@@ -94,11 +124,19 @@
         there = lax.rem(c + o, NC)
         return there, (r, there)
 
+    start_copy = pltpu.make_async_copy(start_hbm, start_ref, copy_sem.at[0])
+    start_copy.start()
+    blocks_copy = pltpu.make_async_copy(blocks_hbm, blocks_ref, copy_sem.at[1])
+    blocks_copy.start()
+
     barrier = pltpu.get_barrier_semaphore()
     for o in range(1, 16):
         pl.semaphore_signal(barrier, inc=1, device_id=along_z(o)[1], device_id_type=MESH)
         pl.semaphore_signal(barrier, inc=1, device_id=along_c(o)[1], device_id_type=MESH)
     pl.semaphore_signal(barrier, inc=1, device_id=sibling, device_id_type=MESH)
+    for o in range(1, 8):
+        there = (sibling[0], ch * 8 + lax.rem(cp + o, 8))
+        pl.semaphore_signal(barrier, inc=1, device_id=there, device_id_type=MESH)
 
     def push(src, dst, send, recv, where):
         pltpu.make_async_remote_copy(
@@ -120,12 +158,13 @@
         total = ar1[s, 0]
         for i in range(1, 16):
             total = total + ar1[s, i]
-        ar_s1[s] = total
-        push(ar_s1.at[s], ar2.at[s], ar_send.at[s, 1], ar_recv.at[s, 1], sibling)
+        ar_s1[s, 0] = total[0:4]
+        ar_s1[s, 1] = total[4:8]
+        push(ar_s1.at[s, 1 - k], ar2.at[s], ar_send.at[s, 1], ar_recv.at[s, 1], sibling)
 
     def reduce_3(s):
         settle(ar2.at[s], ar_recv.at[s, 1])
-        ar_s2[s] = ar_s1[s] + ar2[s]
+        ar_s2[s] = ar_s1[s, k] + ar2[s]
         ar3[s, z] = ar_s2[s]
         for o in FAR:
             push(ar_s2.at[s], ar3.at[s, z], ar_send.at[s, 2], ar_recv.at[s, 2], along_z(o)[1])
@@ -136,20 +175,23 @@
         for i in range(1, 16):
             total = total + ar3[s, i]
         ar_s3[s] = total
-        ar4[s, cp] = total
-        for o in range(1, 8):
+        ar4[s, cp, k] = total
+        for o in range(8):
             there = ch * 8 + lax.rem(cp + o, 8)
-            push(ar_s3.at[s], ar4.at[s, cp], ar_send.at[s, 3], ar_recv.at[s, 3], (r, there))
+            for row in (r, sibling[0]) if o else (sibling[0],):
+                push(ar_s3.at[s], ar4.at[s, cp, k], ar_send.at[s, 3], ar_recv.at[s, 3], (row, there))
 
     def reduce_5(s):
-        settle(ar4.at[s, pl.ds(0, 7)], ar_recv.at[s, 3])
-        x_ref[...] = ar4[s].reshape(64, 128) * (1.0 / (512 * 128))
+        settle(ar3.at[s, pl.ds(0, 15)], ar_recv.at[s, 3])
+        for i in range(8):
+            for h in range(2):
+                x_ref[8 * i + 4 * h : 8 * i + 4 * h + 4] = ar4[s, i, h] * (1.0 / (512 * 128))
 
     def reduce_end(s):
         settle(ar1.at[s, pl.ds(0, 15)], ar_send.at[s, 0])
         settle(ar2.at[s], ar_send.at[s, 1])
         settle(ar3.at[s, pl.ds(0, 15)], ar_send.at[s, 2])
-        settle(ar4.at[s, pl.ds(0, 7)], ar_send.at[s, 3])
+        settle(ar3.at[s, pl.ds(0, 15)], ar_send.at[s, 3])
 
     def spread(t, value):
         u = buffers[t]
@@ -184,14 +226,14 @@
         dims = (((1,), (1,)), ((), ())) if transposed else (((1,), (0,)), ((), ()))
 
         def one(p, total):
-            value = source[plan[base + 64 + p]]
-            matrix = blocks_ref[plan[base + p]]
+            value = source[plan[base + 2, p]]
+            matrix = blocks_ref[plan[base, p]]
             high = value.astype(BF16)
             part = lax.dot_general(high, matrix, dims, preferred_element_type=F32)
             if value.dtype == F32:
                 low = (value - high.astype(F32)).astype(BF16)
                 part = part + lax.dot_general(low, matrix, dims, preferred_element_type=F32)
-            total = jnp.where(plan[base + 32 + p] > 0, total, 0.0) + part
+            total = jnp.where(plan[base + 1, p] > 0, total, 0.0) + part
             sums[p] = total
             return total
 
@@ -201,20 +243,20 @@
         u = buffers[t]
         kind = u["src"].dtype
         settle(u["stripe"].at[pl.ds(0, 15)], u["recv"].at[3])
-        products(128, u["stripe"], False)
+        products(4, u["stripe"], False)
         for i in range(NZ):
-            u["pair_src"][i] = sums[plan[224 + other + i]].astype(kind)
+            u["pair_src"][i] = sums[plan[7, other + i]].astype(kind)
         push(u["pair_src"], u["pair_dst"], u["send"].at[5], u["recv"].at[5], sibling)
         settle(u["pair_dst"], u["recv"].at[5])
         for i in range(15, 4, -1):
-            u["zed_src"][i] = (sums[plan[224 + mine + i]] + u["pair_dst"][i].astype(F32)).astype(kind)
+            u["zed_src"][i] = (sums[plan[7, mine + i]] + u["pair_dst"][i].astype(F32)).astype(kind)
             if i == 11:
                 push(u["zed_src"].at[pl.ds(11, 5)], u["near"].at[pl.ds(0, 5)], u["send"].at[6], u["recv"].at[6], along_z(1)[1])
             if i == 6:
                 push(u["zed_src"].at[pl.ds(6, 5)], u["near"].at[pl.ds(5, 5)], u["send"].at[6], u["recv"].at[6], along_z(-1)[1])
         push(u["zed_src"].at[5], u["far"].at[4], u["send"].at[7], u["recv"].at[7], along_z(8)[1])
         for i in range(5):
-            held[i] = sums[plan[224 + mine + i]] + u["pair_dst"][i].astype(F32)
+            held[i] = sums[plan[7, mine + i]] + u["pair_dst"][i].astype(F32)
 
     def forward(t):
         u = buffers[t]
@@ -222,7 +264,7 @@
         products(0, u["colset"], True)
         for o in range(1, 16):
             there, where = along_c(o)
-            u["row_src"][there] = sums[plan[96 + there]].astype(u["src"].dtype)
+            u["row_src"][there] = sums[plan[3, there]].astype(u["src"].dtype)
             push(u["row_src"].at[there], u["row_dst"].at[c], u["send"].at[8], u["recv"].at[8], where)
 
     def pass_on(t):
@@ -235,7 +277,7 @@
 
     def collect(t):
         u = buffers[t]
-        total = held[0] + u["near"][0].astype(F32) + u["near"][5].astype(F32) + sums[plan[96 + c]]
+        total = held[0] + u["near"][0].astype(F32) + u["near"][5].astype(F32) + sums[plan[3, c]]
         settle(u["row_dst"].at[pl.ds(0, 15)], u["recv"].at[8])
         for i in range(NC):
             total = total + u["row_dst"][i].astype(F32)
@@ -273,9 +315,11 @@
         return alpha_t
 
     sums[SLOTS] = jnp.zeros((64, 128), F32)
+    start_copy.wait()
     first = start_ref[...]
     x_ref[...] = nt(first, jnp.concatenate([first, first], axis=0))
-    pl.semaphore_wait(barrier, 31)
+    blocks_copy.wait()
+    pl.semaphore_wait(barrier, 38)
 
     for s in range(ITERS):
         if s:
@@ -323,20 +367,21 @@
     reduce_end(ITERS)
 
 
+def finish(basis_ref, alpha_ref, beta_ref, basis_out, alpha_out, beta_out):
+    basis_out[...] = basis_ref[...]
+    for t in range(ITERS):
+        alpha_out[t] = alpha_ref[t].T
+        beta_out[t] = beta_ref[t].T
+
+
 def shards(blocks, block_rows, block_cols, start):
-    row_index = lax.axis_index("row")
-    valid = block_rows < 512
-    row_target = block_rows - row_index * NC
-    col_owner = block_cols // NC
-    away = lax.rem(col_owner // 2 - row_index // 2 + 3 * NZ, NZ)
-    slot = jnp.sum(jnp.where(away[:, None] == jnp.array(REACH)[None, :], jnp.arange(NZ)[None, :], 0), axis=1)
-    col_target = lax.rem(col_owner, 2) * NZ + slot
-    plan = jnp.concatenate(
-        plan_part(row_target, col_target, valid, NC) + plan_part(col_target, row_target, valid, 2 * NZ)
+    vmem = pl.BlockSpec(memory_space=pltpu.VMEM)
+    shapes = (
+        jax.ShapeDtypeStruct((64, 128), F32),
+        jax.ShapeDtypeStruct((ITERS, 64, 64), F32),
+        jax.ShapeDtypeStruct((ITERS, 64, 64), F32),
     )
-    vmem = pl.BlockSpec(memory_space=pltpu.VMEM)
-    tall = (ITERS + 1, 16, 8, 128)
-    piece = (ITERS + 1, 8, 128)
+    half = (ITERS + 1, 4, 128)
 
     def buffer(kind):
         counts = dict(
@@ -348,16 +393,23 @@
         made["recv"] = pltpu.SemaphoreType.DMA((9,))
         return made
 
+    plan = pl.pallas_call(
+        make_plan,
+        out_shape=jax.ShapeDtypeStruct((8, 128), jnp.int32),
+        in_specs=[vmem, vmem],
+        out_specs=vmem,
+        compiler_params=pltpu.CompilerParams(vmem_limit_bytes=60 << 20),
+        name="plan",
+    )(block_rows.reshape(1, SLOTS), block_cols.reshape(1, SLOTS))
     basis, alphas, betas = pl.pallas_call(
         kernel,
-        out_shape=(
-            jax.ShapeDtypeStruct((64, 128), F32),
-            jax.ShapeDtypeStruct((ITERS, 64, 64), F32),
-            jax.ShapeDtypeStruct((ITERS, 64, 64), F32),
-        ),
-        in_specs=[pl.BlockSpec(memory_space=pltpu.SMEM), vmem, vmem],
+        out_shape=shapes,
+        in_specs=[pl.BlockSpec(memory_space=pltpu.SMEM), HBM, HBM],
         out_specs=(vmem, vmem, vmem),
         scratch_shapes=[
+            pltpu.VMEM((64, 128), F32),
+            pltpu.VMEM((SLOTS, 128, 128), BF16),
+            pltpu.SemaphoreType.DMA((2,)),
             pltpu.VMEM((64, 128), F32),
             pltpu.VMEM((64, 128), F32),
             pltpu.VMEM((64, 128), F32),
@@ -367,20 +419,26 @@
             pltpu.VMEM((5, 64, 128), F32),
             [buffer(F32), buffer(BF16), buffer(BF16)],
             pltpu.VMEM((ITERS + 1, 8, 8, 128), F32),
-            pltpu.VMEM(tall, F32),
-            pltpu.VMEM(piece, F32),
-            pltpu.VMEM(piece, F32),
-            pltpu.VMEM(piece, F32),
-            pltpu.VMEM(tall, F32),
-            pltpu.VMEM(piece, F32),
-            pltpu.VMEM((ITERS + 1, 8, 8, 128), F32),
+            pltpu.VMEM((ITERS + 1, 16, 8, 128), F32),
+            pltpu.VMEM((ITERS + 1, 2, 4, 128), F32),
+            pltpu.VMEM(half, F32),
+            pltpu.VMEM(half, F32),
+            pltpu.VMEM((ITERS + 1, 16, 4, 128), F32),
+            pltpu.VMEM(half, F32),
+            pltpu.VMEM((ITERS + 1, 8, 2, 4, 128), F32),
             pltpu.SemaphoreType.DMA((ITERS + 1, 4)),
             pltpu.SemaphoreType.DMA((ITERS + 1, 4)),
         ],
-        compiler_params=pltpu.CompilerParams(collective_id=0, has_side_effects=True, vmem_limit_bytes=36 << 20),
+        compiler_params=pltpu.CompilerParams(collective_id=0, has_side_effects=True, vmem_limit_bytes=60 << 20),
         name="lanczos",
     )(plan, start, blocks)
-    return (basis, jnp.swapaxes(alphas, 1, 2), jnp.swapaxes(betas, 1, 2))
+    return pl.pallas_call(
+        finish,
+        out_shape=shapes,
+        in_specs=[vmem] * 3,
+        out_specs=(vmem,) * 3,
+        name="finish",
+    )(basis, alphas, betas)
 
 
 def solution(mesh):

time: 123 us -> 119 us (0.967)
  local copies, waits for them, and re-layouts: 5.36 us -> 0 us
  Pallas kernels: 116 us -> 118 us
    unnamed x13 -> x0, local copies, waits for them, and re-layouts: 5.28 us -> none
    pallas_call x1 -> x3, Pallas kernels: 116 us -> 118 us  [the longest x1 115 us: shards(): pl.pallas_call(kernel, out_shape=shapes, in_specs=[pl.BlockSpec(memory_sp...]
where the time goes in v3:
time: 119 us
  Pallas kernels  118 us (99%)
    pallas_call x1, Pallas kernels, shards(): pl.pallas_call(kernel, out_shape=shapes, in_specs=[pl.BlockSpec(memory_sp...  115 us

profile of v3, /device:TPU:1, one launch (start us, length us, event | category | flops | bytes accessed | tf_op | source)
XLA Modules:
  0.0 118.7 jit_solution(15550519862288696971)
XLA Ops:
  0.6 1.5 %plan.1 = s32[8,128]{1,0:T(8,128)} custom-call(s32[1,32]{1,0:T(1,128)} %bitcast.2, s32[1,32]{1,0:T(1,128)} %bitcast.3), custom_call_target="tpu_custom_call" | custom-call | tf_op jit(solution)/shard_map/plan/pallas_call | solution.py:396
  2.1 114.8 %lanczos.1 = (f32[64,128]{1,0:T(8,128)}, f32[3,64,64]{2,1,0:T(8,128)}, f32[3,64,64]{2,1,0:T(8,128)}) custom-call(s32[8,128]{1,0:T(8,128)} %plan.1, f32[64,128]{1,0:T(8,128)} %start_hbm.1, bf16[32,128,128]{2,1,0:T(8,128)(2,1)} %blocks_hbm.1), custom_call_target="tpu_custom_call" | custom-call | tf_op jit(solution)/shard_map/lanczos/pallas_call | solution.py:404
  116.9 1.7 %finish.1 = (f32[64,128]{1,0:T(8,128)}, f32[3,64,64]{2,1,0:T(8,128)}, f32[3,64,64]{2,1,0:T(8,128)}) custom-call(f32[64,128]{1,0:T(8,128)} %get-tuple-element.6.basis_ref, f32[3,64,64]{2,1,0:T(8,128)} %get-tuple-element.7.alpha_ref, f32[3,64,64]{2,1,0:T(8,128)} %get-tuple-element.8.beta_ref), custom_call_target="tpu_custom_call" | custom-call | tf_op jit(solution)/shard_map/finish/pallas_call | solution.py:435

commit v4 on v3

--- a/solution.py
+++ b/solution.py
@@ -28,50 +28,28 @@
 
 
 def plan_part(target, source, valid, targets):
-    across = lax.broadcasted_iota(jnp.int32, (SLOTS, SLOTS), 1).astype(F32)
-    down = lax.broadcasted_iota(jnp.int32, (SLOTS, SLOTS), 0).astype(F32)
+    across = lax.broadcasted_iota(jnp.int32, (SLOTS, SLOTS), 1)
+    down = lax.broadcasted_iota(jnp.int32, (SLOTS, SLOTS), 0)
     diagonal = across == down
 
     def upright(row):
-        return jnp.sum(jnp.where(diagonal, row, 0.0), axis=1, keepdims=True)
-
-    target = jnp.where(valid, target, float(targets))
+        return jnp.sum(jnp.where(diagonal, row, 0), axis=1, keepdims=True)
+
+    def pick(column, place):
+        return jnp.sum(jnp.where(place, column, 0), axis=0, keepdims=True)
+
+    target = jnp.where(valid, target, targets)
     key = target * SLOTS + across[:1]
     key_down, target_down = upright(key), upright(target)
-    source_down = upright(jnp.where(valid, source, 0.0))
-    rank = jnp.sum(jnp.where(key < key_down, 1.0, 0.0), axis=1, keepdims=True)
-
-    def pick(column, place):
-        return jnp.sum(jnp.where(place, column, 0.0), axis=0, keepdims=True)
-
+    source_down = upright(jnp.where(valid, source, 0))
+    rank = jnp.sum(jnp.where(key < key_down, 1, 0), axis=1, keepdims=True)
     here = rank == across
     one = jnp.ones_like(rank)
-    same = pick(target_down + 1.0, here) == pick(target_down + 1.0, rank + 1.0 == across)
-    upto = pick(one, key_down < (across + 1.0) * SLOTS)
+    same = pick(target_down + 1, here) == pick(target_down + 1, rank + 1 == across)
+    upto = pick(one, key_down < (across + 1) * SLOTS)
     some = pick(one, target_down == across)
-    last = jnp.where(some > 0.0, upto - 1.0, float(SLOTS))
-    rows = (pick(down[:, :1], here), jnp.where(same, 1.0, 0.0), pick(source_down, here), last)
-    return [row.astype(jnp.int32) for row in rows]
-
-
-def make_plan(rows_ref, cols_ref, plan_ref):
-    r = lax.axis_index("row")
-    z = r // 2
-    row_index, col_index = rows_ref[...], cols_ref[...]
-    valid = row_index < 512
-    owner = lax.shift_right_logical(col_index, 4)
-    away = (lax.shift_right_logical(owner, 1) - z + NZ) & 15
-    slot = jnp.zeros_like(away)
-    for i in range(1, NZ):
-        slot = jnp.where(away == REACH[i], i, slot)
-    row_target = jnp.clip(row_index - r * NC, 0, NC - 1).astype(F32)
-    col_target = ((owner & 1) * NZ + slot).astype(F32)
-    for base, part in (
-        (0, plan_part(row_target, col_target, valid, SLOTS)),
-        (4, plan_part(col_target, row_target, valid, SLOTS)),
-    ):
-        for i in range(4):
-            plan_ref[base + i : base + i + 1, 0:SLOTS] = part[i]
+    last = jnp.where(some > 0, upto - 1, SLOTS)
+    return (pick(down[:, :1], here), jnp.where(same, 1, 0), pick(source_down, here), last)
 
 
 def factor(m_ref):
@@ -105,8 +83,8 @@
 
 
 def kernel(
-    plan, start_hbm, blocks_hbm, basis_ref, alpha_ref, beta_ref,
-    start_ref, blocks_ref, copy_sem, q_ref, y_ref, r_ref, x_ref, m_ref, sums, held, buffers,
+    rows_ref, cols_ref, start_hbm, blocks_hbm, basis_ref, alpha_ref, beta_ref,
+    start_ref, blocks_ref, plan_ref, table, copy_sem, q_ref, y_ref, r_ref, x_ref, m_ref, sums, held, buffers,
     ar_src, ar1, ar_s1, ar2, ar_s2, ar3, ar_s3, ar4, ar_send, ar_recv,
 ):
     r = lax.axis_index("row")
@@ -137,6 +115,9 @@
     for o in range(1, 8):
         there = (sibling[0], ch * 8 + lax.rem(cp + o, 8))
         pl.semaphore_signal(barrier, inc=1, device_id=there, device_id_type=MESH)
+
+    def plan(row, i):
+        return jnp.clip(table[row, i], 0, {3: SLOTS, 6: NC - 1, 7: SLOTS}.get(row, SLOTS - 1))
 
     def push(src, dst, send, recv, where):
         pltpu.make_async_remote_copy(
@@ -226,14 +207,14 @@
         dims = (((1,), (1,)), ((), ())) if transposed else (((1,), (0,)), ((), ()))
 
         def one(p, total):
-            value = source[plan[base + 2, p]]
-            matrix = blocks_ref[plan[base, p]]
+            value = source[plan(base + 2, p)]
+            matrix = blocks_ref[plan(base, p)]
             high = value.astype(BF16)
             part = lax.dot_general(high, matrix, dims, preferred_element_type=F32)
             if value.dtype == F32:
                 low = (value - high.astype(F32)).astype(BF16)
                 part = part + lax.dot_general(low, matrix, dims, preferred_element_type=F32)
-            total = jnp.where(plan[base + 1, p] > 0, total, 0.0) + part
+            total = jnp.where(plan(base + 1, p) > 0, total, 0.0) + part
             sums[p] = total
             return total
 
@@ -245,18 +226,18 @@
         settle(u["stripe"].at[pl.ds(0, 15)], u["recv"].at[3])
         products(4, u["stripe"], False)
         for i in range(NZ):
-            u["pair_src"][i] = sums[plan[7, other + i]].astype(kind)
+            u["pair_src"][i] = sums[plan(7, other + i)].astype(kind)
         push(u["pair_src"], u["pair_dst"], u["send"].at[5], u["recv"].at[5], sibling)
         settle(u["pair_dst"], u["recv"].at[5])
         for i in range(15, 4, -1):
-            u["zed_src"][i] = (sums[plan[7, mine + i]] + u["pair_dst"][i].astype(F32)).astype(kind)
+            u["zed_src"][i] = (sums[plan(7, mine + i)] + u["pair_dst"][i].astype(F32)).astype(kind)
             if i == 11:
                 push(u["zed_src"].at[pl.ds(11, 5)], u["near"].at[pl.ds(0, 5)], u["send"].at[6], u["recv"].at[6], along_z(1)[1])
             if i == 6:
                 push(u["zed_src"].at[pl.ds(6, 5)], u["near"].at[pl.ds(5, 5)], u["send"].at[6], u["recv"].at[6], along_z(-1)[1])
         push(u["zed_src"].at[5], u["far"].at[4], u["send"].at[7], u["recv"].at[7], along_z(8)[1])
         for i in range(5):
-            held[i] = sums[plan[7, mine + i]] + u["pair_dst"][i].astype(F32)
+            held[i] = sums[plan(7, mine + i)] + u["pair_dst"][i].astype(F32)
 
     def forward(t):
         u = buffers[t]
@@ -264,7 +245,7 @@
         products(0, u["colset"], True)
         for o in range(1, 16):
             there, where = along_c(o)
-            u["row_src"][there] = sums[plan[3, there]].astype(u["src"].dtype)
+            u["row_src"][there] = sums[plan(3, there)].astype(u["src"].dtype)
             push(u["row_src"].at[there], u["row_dst"].at[c], u["send"].at[8], u["recv"].at[8], where)
 
     def pass_on(t):
@@ -277,7 +258,7 @@
 
     def collect(t):
         u = buffers[t]
-        total = held[0] + u["near"][0].astype(F32) + u["near"][5].astype(F32) + sums[plan[3, c]]
+        total = held[0] + u["near"][0].astype(F32) + u["near"][5].astype(F32) + sums[plan(3, c)]
         settle(u["row_dst"].at[pl.ds(0, 15)], u["recv"].at[8])
         for i in range(NC):
             total = total + u["row_dst"][i].astype(F32)
@@ -315,10 +296,29 @@
         return alpha_t
 
     sums[SLOTS] = jnp.zeros((64, 128), F32)
+    plan_ref[...] = jnp.zeros((8, 128), jnp.int32)
+    row_index, col_index = rows_ref[...], cols_ref[...]
+    valid = row_index < 512
+    owner = lax.shift_right_logical(col_index, 4)
+    away = (lax.shift_right_logical(owner, 1) - z + NZ) & 15
+    slot = jnp.zeros_like(away)
+    for i in range(1, NZ):
+        slot = jnp.where(away == REACH[i], i, slot)
+    row_target = jnp.clip(row_index - r * NC, 0, NC - 1)
+    col_target = (owner & 1) * NZ + slot
+    for base, part in (
+        (0, plan_part(row_target, col_target, valid, SLOTS)),
+        (4, plan_part(col_target, row_target, valid, SLOTS)),
+    ):
+        for i in range(4):
+            plan_ref[base + i : base + i + 1, 0:SLOTS] = part[i]
+    plan_copy = pltpu.make_async_copy(plan_ref, table, copy_sem.at[2])
+    plan_copy.start()
     start_copy.wait()
     first = start_ref[...]
     x_ref[...] = nt(first, jnp.concatenate([first, first], axis=0))
     blocks_copy.wait()
+    plan_copy.wait()
     pl.semaphore_wait(barrier, 38)
 
     for s in range(ITERS):
@@ -393,23 +393,17 @@
         made["recv"] = pltpu.SemaphoreType.DMA((9,))
         return made
 
-    plan = pl.pallas_call(
-        make_plan,
-        out_shape=jax.ShapeDtypeStruct((8, 128), jnp.int32),
-        in_specs=[vmem, vmem],
-        out_specs=vmem,
-        compiler_params=pltpu.CompilerParams(vmem_limit_bytes=60 << 20),
-        name="plan",
-    )(block_rows.reshape(1, SLOTS), block_cols.reshape(1, SLOTS))
     basis, alphas, betas = pl.pallas_call(
         kernel,
         out_shape=shapes,
-        in_specs=[pl.BlockSpec(memory_space=pltpu.SMEM), HBM, HBM],
+        in_specs=[vmem, vmem, HBM, HBM],
         out_specs=(vmem, vmem, vmem),
         scratch_shapes=[
             pltpu.VMEM((64, 128), F32),
             pltpu.VMEM((SLOTS, 128, 128), BF16),
-            pltpu.SemaphoreType.DMA((2,)),
+            pltpu.VMEM((8, 128), jnp.int32),
+            pltpu.SMEM((8, 128), jnp.int32),
+            pltpu.SemaphoreType.DMA((3,)),
             pltpu.VMEM((64, 128), F32),
             pltpu.VMEM((64, 128), F32),
             pltpu.VMEM((64, 128), F32),
@@ -431,7 +425,7 @@
         ],
         compiler_params=pltpu.CompilerParams(collective_id=0, has_side_effects=True, vmem_limit_bytes=60 << 20),
         name="lanczos",
-    )(plan, start, blocks)
+    )(block_rows.reshape(1, SLOTS), block_cols.reshape(1, SLOTS), start, blocks)
     return pl.pallas_call(
         finish,
         out_shape=shapes,

time: 119 us -> 117 us (0.983)
  Pallas kernels: 118 us -> 116 us
    pallas_call x2 -> x1, Pallas kernels: 116 us -> 114 us  [shards(): pl.pallas_call(kernel, out_shape=shapes, in_specs=[vmem, vmem, HBM, HBM],...]
where the time goes in v4:
time: 117 us
  Pallas kernels  116 us (99%)
    pallas_call x1, Pallas kernels, shards(): pl.pallas_call(kernel, out_shape=shapes, in_specs=[vmem, vmem, HBM, HBM],...  114 us

profile of v4, /device:TPU:1, one launch (start us, length us, event | category | flops | bytes accessed | tf_op | source)
XLA Modules:
  0.0 116.6 jit_solution(8403518990656578714)
XLA Ops:
  0.6 114.2 %lanczos.1 = (f32[64,128]{1,0:T(8,128)}, f32[3,64,64]{2,1,0:T(8,128)}, f32[3,64,64]{2,1,0:T(8,128)}) custom-call(s32[1,32]{1,0:T(1,128)} %bitcast.2, s32[1,32]{1,0:T(1,128)} %bitcast.3, f32[64,128]{1,0:T(8,128)} %start_hbm.1, bf16[32,128,128]{2,1,0:T(8,128)(2,1)} %blocks_hbm.1), custom_call_target="tpu_custom_call" | custom-call | tf_op jit(solution)/shard_map/lanczos/pallas_call | solution.py:396
  114.8 1.7 %finish.1 = (f32[64,128]{1,0:T(8,128)}, f32[3,64,64]{2,1,0:T(8,128)}, f32[3,64,64]{2,1,0:T(8,128)}) custom-call(f32[64,128]{1,0:T(8,128)} %get-tuple-element.6.basis_ref, f32[3,64,64]{2,1,0:T(8,128)} %get-tuple-element.7.alpha_ref, f32[3,64,64]{2,1,0:T(8,128)} %get-tuple-element.8.beta_ref), custom_call_target="tpu_custom_call" | custom-call | tf_op jit(solution)/shard_map/finish/pallas_call | solution.py:429

commit v5 on v4

--- a/solution.py
+++ b/solution.py
@@ -324,8 +324,11 @@
     for s in range(ITERS):
         if s:
             x_ref[...] = nt(r_ref[...], jnp.concatenate([r_ref[...], q_ref[...]], axis=0))
+        if s == 0:
+            spread(s, first)
         reduce_1(s)
-        spread(s, r_ref[...] if s else first)
+        if s:
+            spread(s, r_ref[...])
         hop(s, 1)
         reduce_2(s)
         hop(s, 3)

time: 117 us -> 117 us (level)
  no operation moved by 1% of the time
where the time goes in v5:
time: 117 us
  Pallas kernels  116 us (99%)
    pallas_call x1, Pallas kernels, shards(): pl.pallas_call(kernel, out_shape=shapes, in_specs=[vmem, vmem, HBM, HBM],...  114 us

profile of v5, /device:TPU:1, one launch (start us, length us, event | category | flops | bytes accessed | tf_op | source)
XLA Modules:
  0.0 116.7 jit_solution(9767890602627839966)
XLA Ops:
  0.6 114.3 %lanczos.1 = (f32[64,128]{1,0:T(8,128)}, f32[3,64,64]{2,1,0:T(8,128)}, f32[3,64,64]{2,1,0:T(8,128)}) custom-call(s32[1,32]{1,0:T(1,128)} %bitcast.2, s32[1,32]{1,0:T(1,128)} %bitcast.3, f32[64,128]{1,0:T(8,128)} %start_hbm.1, bf16[32,128,128]{2,1,0:T(8,128)(2,1)} %blocks_hbm.1), custom_call_target="tpu_custom_call" | custom-call | tf_op jit(solution)/shard_map/lanczos/pallas_call | solution.py:399
  114.9 1.7 %finish.1 = (f32[64,128]{1,0:T(8,128)}, f32[3,64,64]{2,1,0:T(8,128)}, f32[3,64,64]{2,1,0:T(8,128)}) custom-call(f32[64,128]{1,0:T(8,128)} %get-tuple-element.6.basis_ref, f32[3,64,64]{2,1,0:T(8,128)} %get-tuple-element.7.alpha_ref, f32[3,64,64]{2,1,0:T(8,128)} %get-tuple-element.8.beta_ref), custom_call_target="tpu_custom_call" | custom-call | tf_op jit(solution)/shard_map/finish/pallas_call | solution.py:432
